TPU v7x, 32 devices: a whole 2x2x4 slice. The times are simulated.
32 devices in a mesh: seq: 16 (over z, y, x), head: 2 (over core).
Axes of the slice: x: 2, y: 2, z: 4, core: 2. Of those that a mesh axis runs over, the one named last changes fastest.
Arguments:
- queries: bfloat16 [4096, 4096], P('seq', 'head'), may hold values from -6 to 6
- keys: bfloat16 [4096, 4096], P('seq', 'head'), may hold values from -6 to 6
- values: bfloat16 [4096, 4096], P('seq', 'head'), may hold values from -6 to 6
- gain: float32 [4096], P('head'), may hold values from 0.1 to 1.9
- w_out: bfloat16 [4096, 3072], P('head', 'seq'), may hold values from -0.09375 to 0.09375
Outputs:
- mixed: bfloat16 [4096, 3072], P(('seq', 'head'))
All inputs are finite; a program needn't handle non-finite values.
Results may differ from a plain program's by a relative error of at most 0.0049.
Values may be sent and summed in bfloat16 or wider, within the bound.
A program may use at most 320 MiB of HBM per device.

v0:
```python
import jax
import jax.numpy as jnp
from jax import lax
from jax.sharding import PartitionSpec as P

DH = 128


def per_device(queries, keys, values, gain, w_out):
    tok_rows = queries.shape[0]
    group_heads = queries.shape[1] // DH
    block_count = tok_rows // DH
    query_blocks = queries.reshape(block_count, DH, group_heads, DH)
    key_blocks = keys.reshape(block_count, DH, group_heads, DH)
    value_blocks = values.reshape(block_count, DH, group_heads, DH)
    highest = lax.Precision.HIGHEST
    block_states = jnp.einsum(
        "bthd,bthe->bhde", key_blocks, value_blocks, preferred_element_type=jnp.float32
    )
    local_state = jnp.sum(block_states, axis=0)
    seq_count = lax.axis_size("seq")
    flattened = local_state.reshape(1, seq_count, -1)
    row_block = lax.all_to_all(flattened, "seq", split_axis=1, concat_axis=0, tiled=True)
    before = jnp.concatenate(
        [jnp.zeros_like(row_block[:1]), jnp.cumsum(row_block[:-1], axis=0)], axis=0
    )
    prior = lax.all_to_all(before, "seq", split_axis=0, concat_axis=1, tiled=True).reshape(
        local_state.shape
    )
    earlier_blocks = jnp.concatenate(
        [jnp.zeros_like(block_states[:1]), jnp.cumsum(block_states[:-1], axis=0)], axis=0
    )
    starts = prior[None] + earlier_blocks
    cross = jnp.einsum(
        "bthd,bhde->bthe", query_blocks.astype(jnp.float32), starts, precision=highest
    )
    scores = jnp.einsum(
        "bthd,bshd->bhts", query_blocks, key_blocks, preferred_element_type=jnp.float32
    )
    causal_mask = jnp.arange(DH)[:, None] >= jnp.arange(DH)[None, :]
    scores = jnp.where(causal_mask[None, None], scores, jnp.float32(0.0))
    inner = jnp.einsum(
        "bhts,bshe->bthe", scores, value_blocks.astype(jnp.float32), precision=highest
    )
    attn = cross + inner
    gain_rows = gain.reshape(group_heads, DH)
    meansq = jnp.mean(attn * attn, axis=-1, keepdims=True)
    normed = (attn * lax.rsqrt(meansq + 1e-06) * gain_rows).astype(jnp.bfloat16)
    normed = normed.reshape(tok_rows, group_heads * DH)
    terms = jnp.dot(
        normed, lax.all_gather(w_out, "seq", axis=1, tiled=True), preferred_element_type=jnp.float32
    )
    return lax.psum_scatter(terms, "head", scatter_dimension=0, tiled=True).astype(jnp.bfloat16)


def solution(mesh):
    return jax.shard_map(
        per_device,
        mesh=mesh,
        in_specs=(
            P("seq", "head"),
            P("seq", "head"),
            P("seq", "head"),
            P("head"),
            P("head", "seq"),
        ),
        out_specs=P(("seq", "head"), None),
        check_vma=False,
    )
```

profile of v0, /device:TPU:11, one launch (start us, length us, event | category | flops | bytes accessed | tf_op | source)
XLA Modules:
  0.0 231.2 jit_solution(4338576072991749320)
XLA Ops:
  6.5 0.0 all-gather.2.cloned.1.call-start
  6.5 0.7 all-gather.2.cloned.1.call-update
  7.3 0.0 copy-start.1
  7.3 1.5 copy.27
  8.8 1.0 copy.23
  9.8 0.0 copy-done.1
  9.8 0.2 copy.26
  10.0 2.3 fusion.22
  12.3 47.0 %all_to_all.21 = f32[1,16,16384]{2,0,1:T(1,128)S(1)} all-to-all(f32[1,16,16384]{2,0,1:T(1,128)S(1)} %bitcast.32), channel_id=1, replica_groups=mesh['seq'=16,'head'=2] {'seq'}, dimensions={1} | all-to-all | bytes 2097152 | tf_op jit(solution)/shard_map/all_to_all | solution.py:23
  59.3 0.7 fusion.13
  60.0 1.8 concatenate.6
  61.8 5.8 %all-to-all-start.1 = ((f32[16,1,16384]{2,1,0:T(1,128)}), f32[16,1,16384]{2,1,0:T(1,128)}, u32[]{:S(2)}, u32[]{:S(2)}) async-start(f32[16,1,16384]{2,1,0:T(1,128)} %concatenate.6), calls=%async_computation.1 | async-start | bytes 2097152 | tf_op jit(solution)/shard_map/all_to_all | solution.py:27
  67.5 0.2 reduce-scatter.2.cloned.1.call-start
  67.8 2.3 %slice.13 = f32[1,16,128,128]{3,2,1,0:T(8,128)} slice(f32[2,16,128,128]{3,2,1,0:T(8,128)} %get-tuple-element.6), slice={[0:1], [0:16], [0:128], [0:128]} | slice | bytes 2097152 | tf_op jit(solution)/shard_map/slice | solution.py:31
  70.1 1.5 copy.28
  71.6 2.2 fusion.16
  73.8 42.3 %all-to-all-done.1 = f32[16,1,16384]{2,1,0:T(1,128)} async-done(((f32[16,1,16384]{2,1,0:T(1,128)}), f32[16,1,16384]{2,1,0:T(1,128)}, u32[]{:S(2)}, u32[]{:S(2)}) %all-to-all-start.1) | async-done | bytes 1048608 | tf_op jit(solution)/shard_map/all_to_all | solution.py:27
  116.1 0.0 copy-start
  116.1 3.6 %fusion.2 = f32[2,16,128,128]{3,2,1,0:T(8,128)S(1)} fusion(f32[1,16,128,128]{3,2,1,0:T(8,128)} %slice.13, f32[16,128,128]{2,1,0:T(8,128)} %bitcast.3, bf16[2,128,16,128]{3,2,1,0:T(8,128)(2,1)S(1)} %bitcast.31), kind=kOutput, calls=%fused_computation.5 | convolution fusion | flops 805830656 | bytes 5242880 | tf_op jit(solution)/shard_map/bthd,bhde->bthe/dot_general | solution.py:34
  119.6 0.0 copy-done
  119.6 0.0 copy-start.2
  119.6 2.4 %multiply_reduce_fusion = (f32[2,128,16]{1,2,0:T(8,128)S(1)}, f32[2,128,16,128]{1,3,2,0:T(8,128)S(1)}) fusion(bf16[2,128,16,128]{1,3,2,0:T(8,128)(2,1)S(1)} %copy.23, f32[2,16,128,128]{3,2,1,0:T(8,128)S(1)} %copy-done, pred[128,128]{1,0:T(8,128)(4,1)S(1)} %iota_compare_fusion, f32[2,16,128,128]{3,2,1,0:T(8,128)S(1)} %fusion.2), kind=kOutput, calls=%fused_computation.2 | convolution fusion | flops 807399424 | bytes 7372800 | tf_op jit(solution)/shard_map/bhts,bshe->bthe/dot_general | solution.py:42
  122.1 0.0 copy-done.2
  122.1 0.4 multiply_convert_fusion
  122.5 1.0 copy.24
  123.5 76.5 %all-gather.2.cloned.1.call-done = bf16[2048,3072]{0,1:T(8,128)(2,1)} async-done(((bf16[2048,192]{0,1:T(8,128)(2,1)}), bf16[2048,3072]{0,1:T(8,128)(2,1)}) %all-gather.2.cloned.1.call-update) | async-done | bytes 12582928 | tf_op jit(solution)/shard_map/all_gather | solution.py:51
  200.0 9.7 %fusion.7 = f32[256,3072]{1,0:T(8,128)} fusion(bf16[2048,3072]{0,1:T(8,128)(2,1)} %all-gather.2.cloned.1.call-done, bf16[32,8,16,128]{3,2,1,0:T(8,128)(2,1)S(1)} %bitcast.38), kind=kOutput, calls=%fused_computation.8 | convolution fusion | flops 3221225472 | bytes 16777216 | tf_op jit(solution)/shard_map/dot_general | solution.py:50
  209.7 0.0 reduce-scatter.2.cloned.1.call-update
  209.7 12.2 %reduce-scatter.2.cloned.1.call-done = f32[128,3072]{1,0:T(8,128)} async-done(((f32[256,3072]{1,0:T(8,128)}), f32[128,3072]{1,0:T(8,128)}) %reduce-scatter.2.cloned.1.call-update) | async-done | bytes 1572880 | tf_op jit(solution)/shard_map/reduce_scatter | solution.py:53
  221.9 2.4 %convert_element_type.9 = bf16[128,3072]{1,0:T(8,128)(2,1)} convert(f32[128,3072]{1,0:T(8,128)} %reduce-scatter.2.cloned.1.call-done) | non-fusion elementwise | flops 393216 | bytes 2359296 | tf_op jit(solution)/shard_map/convert_element_type | solution.py:53
  (2 shorter events, 0.0 us)
Async XLA Ops:
  6.5 193.5 %all-gather.2.cloned.1.call-start = ((), (), s32[]{:S(2)}) async-start(), calls=%async_computation.3 | async-start | bytes 13369344 | tf_op jit(solution)/shard_map/all_gather | solution.py:51
  7.3 2.5 %copy-start.1 = (bf16[256,2048]{1,0:T(8,128)(2,1)S(1)}, bf16[256,2048]{1,0:T(8,128)(2,1)}, u32[]{:S(2)}) copy-start(bf16[256,2048]{1,0:T(8,128)(2,1)} %param.6) | copy-start | bytes 3145732
  61.8 54.3 %all-to-all-start.1 = ((f32[16,1,16384]{2,1,0:T(1,128)}), f32[16,1,16384]{2,1,0:T(1,128)}, u32[]{:S(2)}, u32[]{:S(2)}) async-start(f32[16,1,16384]{2,1,0:T(1,128)} %concatenate.6), calls=%async_computation.1 | async-start | bytes 2097152 | tf_op jit(solution)/shard_map/all_to_all | solution.py:27
  67.5 154.4 %reduce-scatter.2.cloned.1.call-start = ((), (), s32[]{:S(2)}) async-start(), calls=%async_computation.4 | async-start | bytes 4718592 | tf_op jit(solution)/shard_map/reduce_scatter | solution.py:53
  116.1 3.6 %copy-start = (f32[2,16,128,128]{3,2,1,0:T(8,128)S(1)}, f32[2,16,128,128]{3,2,1,0:T(8,128)}, u32[]{:S(2)}) copy-start(f32[2,16,128,128]{3,2,1,0:T(8,128)} %fusion.16) | copy-start | bytes 6291460
  119.6 2.4 %copy-start.2 = (f32[2048]{0:T(1024)S(1)}, f32[2048]{0:T(1024)}, u32[]{:S(2)}) copy-start(f32[2048]{0:T(1024)} %param.8) | copy-start | bytes 24580
Sparse Core Ops, SparseCore 0:
  10.1 189.8 all-gather.1
  209.8 12.0 reduce-scatter.1
where the time goes:
time: 232 us; the launch traced here: 231 us
  waiting for transfers between devices  132 us (57%)
  blocking collectives  47 us (20%)
  matrix products  20.1 us (9%)
  between operations  13.5 us (6%)
  local copies, waits for them, and re-layouts  9.26 us (4%)
  starting transfers between devices  5.98 us (3%)
  other arithmetic  3.48 us (2%)
    all_gather x1, waiting for transfers between devices, per_device(): lax.all_gather(w_out, 'seq', axis=1, tiled=True)  76.5 us
    all_to_all x1, blocking collectives, per_device(): lax.all_to_all(flattened, 'seq', split_axis=1, concat_axis=0, tiled=True)  47 us
    all_to_all x1, waiting for transfers between devices, per_device(): lax.all_to_all(before, 'seq', split_axis=0, concat_axis=1, tiled=True)  42.3 us
    reduce_scatter x1, waiting for transfers between devices, per_device(): lax.psum_scatter(terms, 'head', scatter_dimension=0, tiled=True)  12.2 us
    dot_general x1, matrix products, per_device(): jnp.dot(normed, lax.all_gather(w_out, 'seq', axis=1, tiled=True), preferr...  9.69 us
    all_to_all x1, starting transfers between devices, per_device(): lax.all_to_all(before, 'seq', split_axis=0, concat_axis=1, tiled=True)  5.76 us
  transfers between devices with their start and end apart: 3, of which 3 were waited for; matrix products, arithmetic and copies ran while one was open for 9% of the time, Pallas kernels for 0%

commit v1 on v0

v1 whole, which is shorter than its diff:
```python
import functools

import jax
import jax.numpy as jnp
from jax import lax
from jax.experimental import pallas as pl
from jax.experimental.pallas import tpu as pltpu
from jax.sharding import PartitionSpec as P

DH = 128
GROUP = 4
MESH = pl.DeviceIdType.MESH
F32 = jnp.float32
BF16 = jnp.bfloat16


def dot(a, b, dims=((1,), (0,))):
    return lax.dot_general(a, b, (dims, ((), ())), preferred_element_type=F32)


def head_columns(head):
    return pl.ds(pl.multiple_of(head * DH, DH), DH)


def kernel(
    lines, group, q_ref, k_ref, v_ref, gain_ref, w_ref, out_ref,
    state, state_in, total, before, prior, inner, weights, normed, give, take, ready, landed,
    w_out_sem, w_in_sem, s_out_sem, s_in_sem, t_out_sem, t_in_sem, b_out_sem, b_in_sem,
    n_out_sem, n_in_sem, p_out_sem, p_in_sem, o_out_sem, o_in_sem,
):
    me = lax.axis_index("seq")
    core = lax.axis_index("head")
    line, place = lax.div(me, group), lax.rem(me, group)
    rows, width = q_ref.shape
    part = width // DH // group
    half = rows // 2
    cols = w_ref.shape[1]
    chunk = part * DH

    def at_place(other):
        return (line * group + other, core)

    def at_line(other):
        return (other * group + place, core)

    def peers(mine, count):
        return [lax.rem(mine + step, count) for step in range(1, count)]

    def copy(src, dst, out_sem, in_sem, to):
        return pltpu.make_async_remote_copy(
            src_ref=src, dst_ref=dst, send_sem=out_sem, recv_sem=in_sem, device_id=to, device_id_type=MESH
        )

    near, far = peers(place, group), peers(line, lines)
    twin = (me, 1 - core)
    greeted = [at_place(o) for o in near] + [at_line(o) for o in far] + [twin]
    barrier = pltpu.get_barrier_semaphore()
    for to in greeted:
        pl.semaphore_signal(barrier, inc=1, device_id=to, device_id_type=MESH)
    pl.semaphore_wait(barrier, len(greeted))

    sent = []

    def send(*args):
        started = copy(*args)
        started.start()
        sent.append(started)

    def states_of(owner):
        def body(i, _):
            columns = head_columns(owner * part + i)
            state[owner, i] = dot(k_ref[:, columns], v_ref[:, columns], ((0,), (0,))).astype(BF16)
            return 0

        lax.fori_loop(0, part, body, 0)

    for step, other in enumerate(near):
        states_of(other)
        send(state.at[other], state_in.at[place], s_out_sem.at[step], s_in_sem.at[place], at_place(other))
    for step, other in enumerate(far):
        send(w_ref, weights.at[line], w_out_sem.at[step], w_in_sem.at[line], at_line(other))
    states_of(place)
    state_in[place] = state[place]
    weights[line] = w_ref[...]
    for other in near:
        copy(state.at[other], state_in.at[other], s_out_sem.at[0], s_in_sem.at[other], at_place(other)).wait_recv()
    total[line] = sum(state_in[i].astype(F32) for i in range(group)).astype(BF16)
    for step, other in enumerate(far):
        send(total.at[line], total.at[line], t_out_sem.at[step], t_in_sem.at[line], at_line(other))

    seen = lax.broadcasted_iota(jnp.int32, (rows, rows), 0) >= lax.broadcasted_iota(jnp.int32, (rows, rows), 1)

    def own_tokens(head, _):
        columns = head_columns(head)
        scores = dot(q_ref[:, columns], k_ref[:, columns], ((1,), (1,)))
        scores = jnp.where(seen, scores, 0.0).astype(BF16)
        inner[:, columns] = dot(scores, v_ref[:, columns])
        return 0

    lax.fori_loop(0, width // DH, own_tokens, 0)

    for other in far:
        copy(total.at[other], total.at[other], t_out_sem.at[0], t_in_sem.at[other], at_line(other)).wait_recv()
    running = lax.fori_loop(
        0,
        lines,
        lambda i, acc: acc + jnp.where(i < line, total[i].astype(F32), 0.0),
        jnp.zeros(total.shape[1:], F32),
    )
    for i in range(group):
        before[i] = running.astype(BF16)
        running = running + state_in[i].astype(F32)
    for step, other in enumerate(near):
        send(before.at[other], prior.at[place], b_out_sem.at[step], b_in_sem.at[place], at_place(other))
    prior[place] = before[place]

    def finish(owner, slot):
        def body(i, _):
            columns = head_columns(owner * part + i)
            attn = inner[:, columns] + dot(q_ref[:, columns], prior[owner, i])
            meansq = jnp.mean(attn * attn, axis=-1, keepdims=True)
            result = attn * lax.rsqrt(meansq + 1e-06) * gain_ref[:, columns]
            normed[place, owner, :, head_columns(i)] = result.astype(BF16)
            return 0

        lax.fori_loop(0, part, body, 0)
        for step, other in enumerate(near):
            send(
                normed.at[place, owner], normed.at[place, owner],
                n_out_sem.at[slot, step], n_in_sem.at[place, owner], at_place(other),
            )

    finish(place, 0)
    for slot, other in enumerate(near):
        copy(before.at[other], prior.at[other], b_out_sem.at[0], b_in_sem.at[other], at_place(other)).wait_recv()
        finish(other, slot + 1)

    for other in far:
        copy(w_ref, weights.at[other], w_out_sem.at[0], w_in_sem.at[other], at_line(other)).wait_recv()

    def project(block, first, store):
        picked = pl.ds(pl.multiple_of(first * half, half), half)

        def body(i, _):
            terms = [
                dot(normed[block, j, picked, :], weights[i, j * chunk:(j + 1) * chunk, :]) for j in range(group)
            ]
            store(block, i, sum(terms[1:], terms[0]))
            return 0

        lax.fori_loop(0, lines, body, 0)

    def to_twin(block, i, value):
        give[block, i] = value

    def to_owner(block, i, value):
        ready[block, i] = (value + take[block, i]).astype(BF16)

    blocks = [place] + near
    for step, block in enumerate(blocks):
        if step:
            for j in range(group):
                copy(
                    normed.at[block, j], normed.at[block, j], n_out_sem.at[0, 0], n_in_sem.at[block, j], at_place(block)
                ).wait_recv()
        project(block, 1 - core, to_twin)
        send(give.at[block], take.at[block], p_out_sem.at[step], p_in_sem.at[block], twin)
    for step, block in enumerate(near + [place]):
        copy(give.at[block], take.at[block], p_out_sem.at[0], p_in_sem.at[block], twin).wait_recv()
        project(block, core, to_owner)
        if step < group - 1:
            send(ready.at[block], landed.at[place], o_out_sem.at[step], o_in_sem.at[place], at_place(block))
    landed[place] = ready[place]
    for other in near:
        copy(ready.at[other], landed.at[other], o_out_sem.at[0], o_in_sem.at[other], at_place(other)).wait_recv()
    for i in range(lines):
        for g in range(group):
            start = (i * group + g) * cols
            out_ref[:, start:start + cols] = landed[g, i]
    for started in sent:
        started.wait_send()


def fused(seq_count, queries, keys, values, gain, w_out):
    rows, width = queries.shape
    cols = w_out.shape[1]
    group, lines = GROUP, seq_count // GROUP
    part = width // DH // group
    half = rows // 2
    vmem = pltpu.VMEM
    dma = pltpu.SemaphoreType.DMA
    spec = pl.BlockSpec(memory_space=vmem)
    return pl.pallas_call(
        functools.partial(kernel, lines, group),
        out_shape=jax.ShapeDtypeStruct((half, cols * seq_count), BF16),
        in_specs=[spec] * 5,
        out_specs=spec,
        scratch_shapes=[
            vmem((group, part, DH, DH), BF16),
            vmem((group, part, DH, DH), BF16),
            vmem((lines, part, DH, DH), BF16),
            vmem((group, part, DH, DH), BF16),
            vmem((group, part, DH, DH), BF16),
            vmem((rows, width), F32),
            vmem((lines, width, cols), BF16),
            vmem((group, group, rows, part * DH), BF16),
            vmem((group, lines, half, cols), F32),
            vmem((group, lines, half, cols), F32),
            vmem((group, lines, half, cols), BF16),
            vmem((group, lines, half, cols), BF16),
            dma((lines,)), dma((lines,)),
            dma((group,)), dma((group,)),
            dma((lines,)), dma((lines,)),
            dma((group,)), dma((group,)),
            dma((group, group)), dma((group, group)),
            dma((group,)), dma((group,)),
            dma((group,)), dma((group,)),
        ],
        compiler_params=pltpu.CompilerParams(
            collective_id=0, has_side_effects=True, vmem_limit_bytes=62 * 1024 * 1024
        ),
    )(queries, keys, values, gain.reshape(1, width), w_out)


def solution(mesh):
    return jax.shard_map(
        functools.partial(fused, mesh.shape["seq"]),
        mesh=mesh,
        in_specs=(
            P("seq", "head"),
            P("seq", "head"),
            P("seq", "head"),
            P("head"),
            P("head", "seq"),
        ),
        out_specs=P(("seq", "head"), None),
        check_vma=False,
    )
```

time: 232 us -> 187 us (0.81)
  Pallas kernels: 0 us -> 181 us
  waiting for transfers between devices: 132 us -> 0 us
  blocking collectives: 47 us -> 0 us
  matrix products: 20.1 us -> 0 us
  between operations: 13.5 us -> 0.01 us
  starting transfers between devices: 5.98 us -> 0 us
  local copies, waits for them, and re-layouts: 9.26 us -> 4.29 us
  other arithmetic: 3.48 us -> 0 us
    pallas_call x0 -> x1, Pallas kernels: none -> 181 us  [fused(): pl.pallas_call(functools.partial(kernel, lines, group), out_shape=jax.Sha...]
    all_gather x1 -> x0, waiting for transfers between devices: 76.5 us -> none  [per_device(): lax.all_gather(w_out, 'seq', axis=1, tiled=True)]
    all_to_all x1 -> x0, blocking collectives: 47 us -> none  [per_device(): lax.all_to_all(flattened, 'seq', split_axis=1, concat_axis=0, tiled=True)]
    all_to_all x1 -> x0, waiting for transfers between devices: 42.3 us -> none  [per_device(): lax.all_to_all(before, 'seq', split_axis=0, concat_axis=1, tiled=True)]
    dot_general x5 -> x0, matrix products: 20.1 us -> none  [the longest x1 9.69 us: per_device(): jnp.dot(normed, lax.all_gather(w_out, 'seq', axis=1, tiled=True), preferr...]
    reduce_scatter x1 -> x0, waiting for transfers between devices: 12.2 us -> none  [per_device(): lax.psum_scatter(terms, 'head', scatter_dimension=0, tiled=True)]
    all_to_all x1 -> x0, starting transfers between devices: 5.76 us -> none  [per_device(): lax.all_to_all(before, 'seq', split_axis=0, concat_axis=1, tiled=True)]
    convert_element_type x2 -> x0, other arithmetic: 2.78 us -> none  [the longest x1 2.38 us: per_device(): lax.psum_scatter(terms, 'head', scatter_dimension=0, tiled=True)]
  transfers between devices with their start and end apart: 3 -> 0, of which waited for: 3 -> 0; matrix products, arithmetic and copies ran while one was open for 9% -> 0% of each run, Pallas kernels for 0% -> 0%
where the time goes in v1:
time: 187 us; the launch traced here: 186 us
  Pallas kernels  181 us (97%)
  local copies, waits for them, and re-layouts  4.29 us (2%)
    pallas_call x1, Pallas kernels, fused(): pl.pallas_call(functools.partial(kernel, lines, group), out_shape=jax.Sha...  181 us
    unnamed x2, local copies, waits for them, and re-layouts  4.29 us

profile of v1, /device:TPU:11, one launch (start us, length us, event | category | flops | bytes accessed | tf_op | source)
XLA Modules:
  0.0 185.7 jit_solution(6769968793459433036)
XLA Ops:
  0.0 2.2 %copy.6.w_ref = bf16[2048,192]{1,0:T(8,128)(2,1)} copy(bf16[2048,192]{0,1:T(8,128)(2,1)} %param.9) | data formatting | bytes 1572864 | tf_op args[4]
  2.2 181.4 %shard_map.55 = bf16[128,3072]{1,0:T(8,128)(2,1)} custom-call(bf16[256,2048]{1,0:T(8,128)(2,1)} %q_ref.1, bf16[256,2048]{1,0:T(8,128)(2,1)} %k_ref.1, bf16[256,2048]{1,0:T(8,128)(2,1)} %v_ref.1, f32[1,2048]{1,0:T(1,128)} %bitcast.1, bf16[2048,192]{1,0:T(8,128)(2,1)} %copy.6.w_ref), custom_call_target="tpu_custom_call" | custom-call | tf_op jit(solution)/shard_map/pallas_call | solution.py:193
  183.6 2.1 %copy.8 = bf16[128,3072]{1,0:T(8,128)(2,1)} copy(bf16[128,3072]{1,0:T(8,128)(2,1)} %shard_map.55) | data formatting | bytes 1572864

commit v2 on v1

--- a/solution.py
+++ b/solution.py
@@ -1,4 +1,5 @@
 import functools
+import math
 
 import jax
 import jax.numpy as jnp
@@ -9,6 +10,8 @@
 
 DH = 128
 GROUP = 4
+EARLY = (0,)
+LATER = {0: (1,), 1: (2,), 2: (3,)}
 MESH = pl.DeviceIdType.MESH
 F32 = jnp.float32
 BF16 = jnp.bfloat16
@@ -24,7 +27,7 @@
 
 def kernel(
     lines, group, q_ref, k_ref, v_ref, gain_ref, w_ref, out_ref,
-    state, state_in, total, before, prior, inner, weights, normed, give, take, ready, landed,
+    state, state_in, total, before, prior, inner, packed, weights, normed, keep, give, take, ready, landed,
     w_out_sem, w_in_sem, s_out_sem, s_in_sem, t_out_sem, t_in_sem, b_out_sem, b_in_sem,
     n_out_sem, n_in_sem, p_out_sem, p_in_sem, o_out_sem, o_in_sem,
 ):
@@ -34,7 +37,9 @@
     rows, width = q_ref.shape
     part = width // DH // group
     half = rows // 2
-    cols = w_ref.shape[1]
+    fold = width // w_ref.shape[0]
+    cols = w_ref.shape[1] // fold
+    depth = w_ref.shape[0]
     chunk = part * DH
 
     def at_place(other):
@@ -77,16 +82,27 @@
     for step, other in enumerate(near):
         states_of(other)
         send(state.at[other], state_in.at[place], s_out_sem.at[step], s_in_sem.at[place], at_place(other))
-    for step, other in enumerate(far):
-        send(w_ref, weights.at[line], w_out_sem.at[step], w_in_sem.at[line], at_line(other))
     states_of(place)
     state_in[place] = state[place]
-    weights[line] = w_ref[...]
+    packed[line] = w_ref[...]
     for other in near:
         copy(state.at[other], state_in.at[other], s_out_sem.at[0], s_in_sem.at[other], at_place(other)).wait_recv()
     total[line] = sum(state_in[i].astype(F32) for i in range(group)).astype(BF16)
     for step, other in enumerate(far):
         send(total.at[line], total.at[line], t_out_sem.at[step], t_in_sem.at[line], at_line(other))
+
+    piece = depth // group
+
+    def send_weights(c):
+        picked = pl.ds(c * piece, piece)
+        for step, other in enumerate(far):
+            send(
+                w_ref.at[picked, :], packed.at[line, picked, :],
+                w_out_sem.at[step, c], w_in_sem.at[line, c], at_line(other),
+            )
+
+    for c in EARLY:
+        send_weights(c)
 
     seen = lax.broadcasted_iota(jnp.int32, (rows, rows), 0) >= lax.broadcasted_iota(jnp.int32, (rows, rows), 1)
 
@@ -120,56 +136,60 @@
             attn = inner[:, columns] + dot(q_ref[:, columns], prior[owner, i])
             meansq = jnp.mean(attn * attn, axis=-1, keepdims=True)
             result = attn * lax.rsqrt(meansq + 1e-06) * gain_ref[:, columns]
-            normed[place, owner, :, head_columns(i)] = result.astype(BF16)
+            normed[owner, place, :, head_columns(i)] = result.astype(BF16)
             return 0
 
         lax.fori_loop(0, part, body, 0)
         for step, other in enumerate(near):
             send(
-                normed.at[place, owner], normed.at[place, owner],
+                normed.at[owner, place], normed.at[owner, place],
                 n_out_sem.at[slot, step], n_in_sem.at[place, owner], at_place(other),
             )
+
+        for c in LATER.get(slot, ()):
+            send_weights(c)
 
     finish(place, 0)
     for slot, other in enumerate(near):
         copy(before.at[other], prior.at[other], b_out_sem.at[0], b_in_sem.at[other], at_place(other)).wait_recv()
         finish(other, slot + 1)
 
-    for other in far:
-        copy(w_ref, weights.at[other], w_out_sem.at[0], w_in_sem.at[other], at_line(other)).wait_recv()
-
-    def project(block, first, store):
+    for block in near:
+        for j in range(group):
+            copy(
+                normed.at[j, block], normed.at[j, block], n_out_sem.at[0, 0], n_in_sem.at[block, j], at_place(block)
+            ).wait_recv()
+
+    def project(i, first):
         picked = pl.ds(pl.multiple_of(first * half, half), half)
-
-        def body(i, _):
-            terms = [
-                dot(normed[block, j, picked, :], weights[i, j * chunk:(j + 1) * chunk, :]) for j in range(group)
-            ]
-            store(block, i, sum(terms[1:], terms[0]))
-            return 0
-
-        lax.fori_loop(0, lines, body, 0)
-
-    def to_twin(block, i, value):
-        give[block, i] = value
-
-    def to_owner(block, i, value):
-        ready[block, i] = (value + take[block, i]).astype(BF16)
-
-    blocks = [place] + near
-    for step, block in enumerate(blocks):
+        terms = [
+            dot(normed[j, :, picked, :].reshape(group * half, chunk), weights[j * chunk:(j + 1) * chunk, :])
+            for j in range(group)
+        ]
+        return sum(terms[1:], terms[0]).reshape(group, half, cols)
+
+    def collect(i):
+        copy(give.at[i], take.at[i], p_out_sem.at[0], p_in_sem.at[i], twin).wait_recv()
+        ready[:, i] = (keep[...] + take[i]).astype(BF16)
+
+    order = [line] + far
+    for step, i in enumerate(order):
         if step:
-            for j in range(group):
+            for c in range(group):
+                picked = pl.ds(c * piece, piece)
                 copy(
-                    normed.at[block, j], normed.at[block, j], n_out_sem.at[0, 0], n_in_sem.at[block, j], at_place(block)
+                    w_ref.at[picked, :], packed.at[i, picked, :], w_out_sem.at[0, 0], w_in_sem.at[i, c], at_line(i)
                 ).wait_recv()
-        project(block, 1 - core, to_twin)
-        send(give.at[block], take.at[block], p_out_sem.at[step], p_in_sem.at[block], twin)
-    for step, block in enumerate(near + [place]):
-        copy(give.at[block], take.at[block], p_out_sem.at[0], p_in_sem.at[block], twin).wait_recv()
-        project(block, core, to_owner)
-        if step < group - 1:
-            send(ready.at[block], landed.at[place], o_out_sem.at[step], o_in_sem.at[place], at_place(block))
+        for f in range(fold):
+            weights[f * depth:(f + 1) * depth, :] = packed[i, :, f * cols:(f + 1) * cols]
+        give[i] = project(i, 1 - core)
+        send(give.at[i], take.at[i], p_out_sem.at[step], p_in_sem.at[i], twin)
+        if step:
+            collect(order[step - 1])
+        keep[...] = project(i, core)
+    collect(order[-1])
+    for step, other in enumerate(near):
+        send(ready.at[other], landed.at[place], o_out_sem.at[step], o_in_sem.at[place], at_place(other))
     landed[place] = ready[place]
     for other in near:
         copy(ready.at[other], landed.at[other], o_out_sem.at[0], o_in_sem.at[other], at_place(other)).wait_recv()
@@ -184,6 +204,8 @@
 def fused(seq_count, queries, keys, values, gain, w_out):
     rows, width = queries.shape
     cols = w_out.shape[1]
+    fold = DH // math.gcd(cols, DH)
+    w_out = jnp.concatenate(jnp.split(w_out, fold, axis=0), axis=1)
     group, lines = GROUP, seq_count // GROUP
     part = width // DH // group
     half = rows // 2
@@ -202,18 +224,20 @@
             vmem((group, part, DH, DH), BF16),
             vmem((group, part, DH, DH), BF16),
             vmem((rows, width), F32),
-            vmem((lines, width, cols), BF16),
+            vmem((lines,) + w_out.shape, BF16),
+            vmem((width, cols), BF16),
             vmem((group, group, rows, part * DH), BF16),
-            vmem((group, lines, half, cols), F32),
-            vmem((group, lines, half, cols), F32),
+            vmem((group, half, cols), F32),
+            vmem((lines, group, half, cols), F32),
+            vmem((lines, group, half, cols), F32),
             vmem((group, lines, half, cols), BF16),
             vmem((group, lines, half, cols), BF16),
-            dma((lines,)), dma((lines,)),
+            dma((lines, group)), dma((lines, group)),
             dma((group,)), dma((group,)),
             dma((lines,)), dma((lines,)),
             dma((group,)), dma((group,)),
             dma((group, group)), dma((group, group)),
-            dma((group,)), dma((group,)),
+            dma((lines,)), dma((lines,)),
             dma((group,)), dma((group,)),
         ],
         compiler_params=pltpu.CompilerParams(

time: 187 us -> 123 us (0.66)
  Pallas kernels: 181 us -> 117 us
    pallas_call x1, Pallas kernels: 181 us -> 117 us  [fused(): pl.pallas_call(functools.partial(kernel, lines, group), out_shape=jax.Sha...]
    unnamed x2 -> x3, local copies, waits for them, and re-layouts: 4.29 us -> 2.47 us
where the time goes in v2:
time: 123 us; the launch traced here: 122 us
  Pallas kernels  117 us (95%)
  local copies, waits for them, and re-layouts  3.64 us (3%)
    pallas_call x1, Pallas kernels, fused(): pl.pallas_call(functools.partial(kernel, lines, group), out_shape=jax.Sha...  117 us
    unnamed x3, local copies, waits for them, and re-layouts  2.47 us

profile of v2, /device:TPU:11, one launch (start us, length us, event | category | flops | bytes accessed | tf_op | source)
XLA Modules:
  0.0 122.3 jit_solution(1076517589775770031)
XLA Ops:
  0.0 1.2 fusion
  1.2 0.2 copy.8
  1.4 0.2 copy.9
  1.6 1.2 pad_maximum_fusion.w_ref
  2.8 117.5 %shard_map.55 = bf16[128,3072]{1,0:T(8,128)(2,1)} custom-call(bf16[256,2048]{1,0:T(8,128)(2,1)} %q_ref.1, bf16[256,2048]{1,0:T(8,128)(2,1)} %k_ref.1, bf16[256,2048]{1,0:T(8,128)(2,1)} %v_ref.1, f32[1,2048]{1,0:T(1,128)} %bitcast.1, bf16[1024,384]{1,0:T(8,128)(2,1)} %pad_maximum_fusion.w_ref), custom_call_target="tpu_custom_call" | custom-call | tf_op jit(solution)/shard_map/pallas_call | solution.py:215
  120.3 2.1 %copy.11 = bf16[128,3072]{1,0:T(8,128)(2,1)} copy(bf16[128,3072]{1,0:T(8,128)(2,1)} %shard_map.55) | data formatting | bytes 1572864

commit v3 on v2

--- a/solution.py
+++ b/solution.py
@@ -77,7 +77,7 @@
             state[owner, i] = dot(k_ref[:, columns], v_ref[:, columns], ((0,), (0,))).astype(BF16)
             return 0
 
-        lax.fori_loop(0, part, body, 0)
+        lax.fori_loop(0, part, body, 0, unroll=True)
 
     for step, other in enumerate(near):
         states_of(other)
@@ -113,7 +113,12 @@
         inner[:, columns] = dot(scores, v_ref[:, columns])
         return 0
 
-    lax.fori_loop(0, width // DH, own_tokens, 0)
+    def own_share(share, _):
+        for i in range(part):
+            own_tokens(share * part + i, 0)
+        return 0
+
+    lax.fori_loop(0, group, own_share, 0)
 
     for other in far:
         copy(total.at[other], total.at[other], t_out_sem.at[0], t_in_sem.at[other], at_line(other)).wait_recv()
@@ -139,7 +144,7 @@
             normed[owner, place, :, head_columns(i)] = result.astype(BF16)
             return 0
 
-        lax.fori_loop(0, part, body, 0)
+        lax.fori_loop(0, part, body, 0, unroll=True)
         for step, other in enumerate(near):
             send(
                 normed.at[owner, place], normed.at[owner, place],

time: 123 us -> 122 us (level)
  no operation moved by 1% of the time
where the time goes in v3:
time: 122 us
  Pallas kernels  117 us (96%)
  local copies, waits for them, and re-layouts  3.64 us (3%)
    pallas_call x1, Pallas kernels, fused(): pl.pallas_call(functools.partial(kernel, lines, group), out_shape=jax.Sha...  117 us
    unnamed x3, local copies, waits for them, and re-layouts  2.47 us

profile of v3, /device:TPU:11, one launch (start us, length us, event | category | flops | bytes accessed | tf_op | source)
XLA Modules:
  0.0 121.8 jit_solution(1730263995679201554)
XLA Ops:
  0.0 1.2 fusion
  1.2 0.2 copy.8
  1.4 0.2 copy.9
  1.6 1.2 pad_maximum_fusion.w_ref
  2.8 117.0 %shard_map.55 = bf16[128,3072]{1,0:T(8,128)(2,1)} custom-call(bf16[256,2048]{1,0:T(8,128)(2,1)} %q_ref.1, bf16[256,2048]{1,0:T(8,128)(2,1)} %k_ref.1, bf16[256,2048]{1,0:T(8,128)(2,1)} %v_ref.1, f32[1,2048]{1,0:T(1,128)} %bitcast.1, bf16[1024,384]{1,0:T(8,128)(2,1)} %pad_maximum_fusion.w_ref), custom_call_target="tpu_custom_call" | custom-call | tf_op jit(solution)/shard_map/pallas_call | solution.py:220
  119.7 2.1 %copy.11 = bf16[128,3072]{1,0:T(8,128)(2,1)} copy(bf16[128,3072]{1,0:T(8,128)(2,1)} %shard_map.55) | data formatting | bytes 1572864
